TPU v7x, 32 devices: a whole 2x2x4 slice. The times are simulated.
32 devices in a mesh: ctx: 8 (over y, x, core), head: 4 (over z).
Axes of the slice: x: 2, y: 2, z: 4, core: 2. Of those that a mesh axis runs over, the one named last changes fastest.
Arguments:
- queries: bfloat16 [256, 16384], P('ctx', 'head'), may hold values from -512 to 512
- kv_cache: bfloat16 [2, 4096, 1024], P(None, 'ctx', 'head'), may hold values from -7 to 7
- fill_len: int32 [8], P('ctx'), may hold values from 64 to 512
- prompt_offset: int32 [1], replicated, may hold values from 2048 to 3840
Outputs:
- attended: bfloat16 [256, 16384], P(('ctx', 'head'))
All inputs are finite; a program needn't handle non-finite values.
Results may differ from a plain program's by a relative error of at most 0.0045.
Values may be sent and summed in bfloat16 or wider, within the bound.
A program may use at most 192 MiB of HBM per device.

v0:
```python
import math

import jax
import jax.numpy as jnp
from jax import lax
from jax.sharding import PartitionSpec as P

HEAD_DIM = 128


def shard_partial(query_rows, key_block, value_block, allowed):
    scaling = 1.0 / math.sqrt(query_rows.shape[-1])
    scores = (
        jnp.einsum("nhgd,khd->hgnk", query_rows, key_block, preferred_element_type=jnp.float32)
        * scaling
    )
    scores = jnp.where(allowed[None, None], scores, -1e30)
    row_max = jnp.max(scores, axis=-1)
    weights = jnp.exp(scores - row_max[..., None])
    row_sum = jnp.sum(weights, axis=-1)
    rounded = weights.astype(jnp.bfloat16)
    weighted = jnp.einsum(
        "hgnk,khd->nhgd", rounded, value_block, preferred_element_type=jnp.float32
    )
    weighted = weighted / jnp.transpose(row_sum, (2, 0, 1))[..., None]
    row_count = query_rows.shape[0]
    partial_value = weighted.astype(jnp.bfloat16).reshape(row_count, -1)
    log_total = jnp.transpose(row_max + jnp.log(row_sum), (2, 0, 1)).reshape(row_count, -1)
    return (partial_value, log_total)


def per_device(queries, kv_cache, fill_len, prompt_offset):
    ctx_size = lax.axis_size("ctx")
    ctx_rank = lax.axis_index("ctx")
    slots = kv_cache.shape[1]
    kv_local = kv_cache.shape[2] // HEAD_DIM
    feat_width = queries.shape[1]
    heads_local = feat_width // HEAD_DIM
    groups = heads_local // kv_local
    slot_ids = jnp.arange(slots, dtype=jnp.int32)
    start_pos = prompt_offset[0]
    key_block = kv_cache[0].reshape(slots, kv_local, HEAD_DIM)
    value_block = kv_cache[1].reshape(slots, kv_local, HEAD_DIM)
    key_pos = ctx_rank * slots + slot_ids
    live_slots = slot_ids < fill_len[0]
    arrived = lax.all_gather(queries, "ctx", axis=0, tiled=True)
    row_count = arrived.shape[0]
    query_pos = start_pos + jnp.arange(row_count, dtype=jnp.int32)
    allowed = live_slots[None, :] & (key_pos[None, :] <= query_pos[:, None])
    partial_value, log_total = shard_partial(
        arrived.reshape(row_count, kv_local, groups, HEAD_DIM), key_block, value_block, allowed
    )
    received = lax.all_to_all(
        partial_value[None], ("ctx", "head"), split_axis=1, concat_axis=0, tiled=True
    )
    received_logs = lax.all_to_all(
        log_total[None], ("ctx", "head"), split_axis=1, concat_axis=0, tiled=True
    )
    head_size = lax.axis_size("head")
    token_rows = received.shape[1]
    received = received.reshape(ctx_size, head_size, token_rows, heads_local, HEAD_DIM)
    received_logs = received_logs.reshape(ctx_size, head_size, token_rows, heads_local)
    log_peak = jnp.max(received_logs, axis=0)
    shares = jnp.exp(received_logs - log_peak[None])
    merged = (
        jnp.sum(shares[..., None] * received.astype(jnp.float32), axis=0)
        / jnp.sum(shares, axis=0)[..., None]
    )
    merged = jnp.transpose(merged, (1, 0, 2, 3)).reshape(token_rows, head_size * feat_width)
    return merged.astype(jnp.bfloat16)


def solution(mesh):
    in_specs = (P("ctx", "head"), P(None, "ctx", "head"), P("ctx"), P())
    out_specs = P(("ctx", "head"), None)
    return jax.shard_map(
        per_device, mesh=mesh, in_specs=in_specs, out_specs=out_specs, check_vma=False
    )
```

profile of v0, /device:TPU:1, one launch (start us, length us, event | category | flops | bytes accessed | tf_op | source)
XLA Modules:
  0.0 178.1 jit_solution(1938333532314203344)
XLA Ops:
  6.5 0.0 all-gather.2.cloned.1.call-start
  6.5 0.7 all-gather.2.cloned.1.call-update
  7.3 1.1 fusion.13
  8.3 0.1 copy.36
  9.8 0.1 copy.46
  10.0 0.2 compare_and_fusion
  10.2 29.5 %all-gather.2.cloned.1.call-done = bf16[256,4096]{1,0:T(8,128)(2,1)} async-done(((bf16[32,4096]{1,0:T(8,128)(2,1)}), bf16[256,4096]{1,0:T(8,128)(2,1)}) %all-gather.2.cloned.1.call-update) | async-done | bytes 2097168 | tf_op jit(solution)/shard_map/all_gather | solution.py:46
  39.7 3.3 %copy.32 = bf16[256,4096]{0,1:T(8,128)(2,1)S(1)} copy(bf16[256,4096]{1,0:T(8,128)(2,1)} %all-gather.2.cloned.1.call-done) | data formatting | bytes 4194304 | tf_op jit(solution)/shard_map/all_gather | solution.py:46
  43.0 7.2 %fusion.2 = (f32[2,16,256]{2,1,0:T(8,128)S(1)}, f32[2,512,256,16]{2,1,3,0:T(8,128)}) fusion(pred[256,512]{0,1:T(8,128)(4,1)S(1)} %compare_and_fusion, bf16[512,2,128,1]{0,2,3,1:T(8,128)(2,1)S(1)} %bitcast.62, bf16[256,2,16,128]{0,3,2,1:T(8,128)(2,1)S(1)} %bitcast.56), kind=kOutput, calls=%fused_computation.4 | convolution fusion | flops 1086316544 | bytes 19300352 | tf_op jit(solution)/shard_map/nhgd,khd->hgnk/dot_general | solution.py:14
  50.2 9.3 %fusion.1 = f32[2,16,256]{2,1,0:T(8,128)S(1)} fusion(f32[2,512,256,16]{2,1,3,0:T(8,128)} %get-tuple-element.10, f32[2,16,256]{2,1,0:T(8,128)S(1)} %get-tuple-element.9, pred[256,512]{0,1:T(8,128)(4,1)S(1)} %compare_and_fusion), kind=kLoop, calls=%fused_computation.3 | loop fusion | flops 16769024 | bytes 16973824 | tf_op jit(solution)/shard_map/reduce_sum | solution.py:20
  59.5 0.1 copy.35
  59.6 0.5 broadcast.68
  60.1 0.9 reduce.1
  61.0 0.7 reshape.98
  61.7 4.6 %all-to-all-start = ((f32[32,1,256]{2,1,0:T(1,128)}), f32[32,1,256]{2,1,0:T(1,128)S(1)}, u32[]{:S(2)}, u32[]{:S(2)}) async-start(f32[32,1,256]{2,1,0:T(1,128)} %reshape.98), calls=%async_computation | async-start | bytes 65536 | tf_op jit(solution)/shard_map/all_to_all | solution.py:56
  66.3 10.0 %fusion.6 = bf16[256,2,16,128]{0,3,2,1:T(8,128)(2,1)S(1)} fusion(bf16[512,2,128,1]{0,2,3,1:T(8,128)(2,1)S(1)} %bitcast.65, f32[2,512,256,16]{2,1,3,0:T(8,128)} %get-tuple-element.10, f32[2,16,256]{2,1,0:T(8,128)S(1)} %get-tuple-element.9, pred[256,512]{0,1:T(8,128)(4,1)S(1)} %compare_and_fusion, f32[256,2,16]{0,2,1:T(8,128)S(1)} %bitcast.66), kind=kOutput, calls=%fused_computation.8 | convolution fusion | flops 1092616192 | bytes 19333120 | tf_op jit(solution)/shard_map/hgnk,khd->nhgd/dot_general | solution.py:22
  76.4 7.9 %copy.38 = bf16[1,256,4096]{2,0,1:T(2,128)(2,1)} copy(bf16[1,256,4096]{1,2,0:T(8,128)(2,1)S(1)} %bitcast.59) | data formatting | bytes 4194304 | tf_op jit(solution)/shard_map/broadcast_in_dim;reshape | solution.py:54
  84.2 0.5 broadcast.67
  84.8 13.5 %reduce = bf16[256,4096]{1,0:T(8,128)(2,1)S(1)} reduce(bf16[256,1,4096]{2,1,0:T(2,128)(2,1)} %bitcast.57, bf16[]{:T(256)} %broadcast.67), dimensions={1}, to_apply=%bitcast.45.reduce_sub_computation | reduce | bytes 4194306
  98.2 3.3 %reshape.96 = bf16[32,2,16384]{2,1,0:T(2,128)(2,1)} reshape(bf16[256,4096]{1,0:T(8,128)(2,1)S(1)} %reduce) | data formatting | bytes 4194304
  101.5 0.0 all-to-all-done
  101.5 5.8 %all-to-all-start.1 = ((bf16[32,2,16384]{2,1,0:T(2,128)(2,1)}), bf16[32,2,16384]{2,1,0:T(2,128)(2,1)S(1)}, u32[]{:S(2)}, u32[]{:S(2)}) async-start(bf16[32,2,16384]{2,1,0:T(2,128)(2,1)} %reshape.96), calls=%async_computation.1 | async-start | bytes 4194304 | tf_op jit(solution)/shard_map/all_to_all | solution.py:53
  107.4 0.6 reduce.2
  108.0 0.2 reshape.99
  108.3 47.3 %all-to-all-done.1 = bf16[32,2,16384]{2,1,0:T(2,128)(2,1)S(1)} async-done(((bf16[32,2,16384]{2,1,0:T(2,128)(2,1)}), bf16[32,2,16384]{2,1,0:T(2,128)(2,1)S(1)}, u32[]{:S(2)}, u32[]{:S(2)}) %all-to-all-start.1) | async-done | bytes 2097184 | tf_op jit(solution)/shard_map/all_to_all | solution.py:53
  155.6 6.8 %reshape.97 = bf16[256,1,4096]{2,1,0:T(2,128)(2,1)} reshape(bf16[32,2,16384]{2,1,0:T(2,128)(2,1)S(1)} %all-to-all-done.1) | data formatting | bytes 4194304
  162.4 6.5 %bitcast_convert_fusion = f32[1,256,4096]{2,0,1:T(1,128)S(1)} fusion(bf16[256,1,4096]{2,1,0:T(2,128)(2,1)} %reshape.97), kind=kLoop, calls=%fused_computation.23 | loop fusion | flops 1048576 | bytes 6291456 | tf_op jit(solution)/shard_map/convert_element_type | solution.py:66
  168.9 1.3 multiply_reduce_fusion
  170.2 0.2 fusion.9
  170.4 0.9 copy.49
  (7 shorter events, 0.1 us)
Async XLA Ops:
  6.5 33.1 %all-gather.2.cloned.1.call-start = ((), (), s32[]{:S(2)}) async-start(), calls=%async_computation.2 | async-start | bytes 2359296 | tf_op jit(solution)/shard_map/all_gather | solution.py:46
  61.7 39.8 %all-to-all-start = ((f32[32,1,256]{2,1,0:T(1,128)}), f32[32,1,256]{2,1,0:T(1,128)S(1)}, u32[]{:S(2)}, u32[]{:S(2)}) async-start(f32[32,1,256]{2,1,0:T(1,128)} %reshape.98), calls=%async_computation | async-start | bytes 65536 | tf_op jit(solution)/shard_map/all_to_all | solution.py:56
  101.5 54.1 %all-to-all-start.1 = ((bf16[32,2,16384]{2,1,0:T(2,128)(2,1)}), bf16[32,2,16384]{2,1,0:T(2,128)(2,1)S(1)}, u32[]{:S(2)}, u32[]{:S(2)}) async-start(bf16[32,2,16384]{2,1,0:T(2,128)(2,1)} %reshape.96), calls=%async_computation.1 | async-start | bytes 4194304 | tf_op jit(solution)/shard_map/all_to_all | solution.py:53
Sparse Core Ops, SparseCore 0:
  9.2 30.3 all-gather.1
where the time goes:
time: 179 us; the launch traced here: 178 us
  waiting for transfers between devices  77.5 us (43%)
  other arithmetic  32.6 us (18%)
  local copies, waits for them, and re-layouts  25.5 us (14%)
  matrix products  17.2 us (10%)
  between operations  14.9 us (8%)
  starting transfers between devices  10.4 us (6%)
    all_to_all x1, waiting for transfers between devices, per_device(): lax.all_to_all(partial_value[None], ('ctx', 'head'), split_axis=1, concat...  47.3 us
    all_gather x1, waiting for transfers between devices, per_device(): arrived = lax.all_gather(queries, 'ctx', axis=0, tiled=True)  29.5 us
    unnamed x2, other arithmetic  14.4 us
    unnamed x8, local copies, waits for them, and re-layouts  13 us
    dot_general x1, matrix products, shard_partial(): jnp.einsum('hgnk,khd->nhgd', rounded, value_block, preferred_element_type...  10 us
    reduce_sum x1, other arithmetic, shard_partial(): row_sum = jnp.sum(weights, axis=-1)  9.31 us
    another operation x1, local copies, waits for them, and re-layouts, per_device(): partial_value[None]  7.88 us
    dot_general x1, matrix products, shard_partial(): jnp.einsum('nhgd,khd->hgnk', query_rows, key_block, preferred_element_typ...  7.2 us
  transfers between devices with their start and end apart: 3, of which 2 were waited for; matrix products, arithmetic and copies ran while one was open for 21% of the time, Pallas kernels for 0%

commit v1 on v0

v1 whole, which is shorter than its diff:
```python
import functools
import math

import jax
import jax.numpy as jnp
from jax import lax
from jax.experimental import pallas as pl
from jax.experimental.pallas import tpu as pltpu
from jax.sharding import PartitionSpec as P

HEAD_DIM = 128
MESH = pl.DeviceIdType.MESH
FILL_ROWS = 16
NEG = -1e30


def xor(a, b, size):
    total = 0
    bit = 1
    while bit < size:
        total = total + lax.rem(lax.rem(lax.div(a, bit), 2) + lax.rem(lax.div(b, bit), 2), 2) * bit
        bit *= 2
    return total


def kernel(
    n_ctx, n_head, fill_ref, offset_ref, q_ref, kv_ref, out_ref,
    buf, other, qbuf, qt, acc, peak, total, staged, landed,
    local_sem, q_send, q_recv, kv_send, kv_recv, out_send, out_recv,
):
    ctx = lax.axis_index("ctx")
    head = lax.axis_index("head")
    core = lax.rem(ctx, 2)
    mate = 1 - core
    group = lax.div(ctx, 2)
    n_group = n_ctx // 2
    slots = kv_ref.shape[1]
    tokens = q_ref.shape[0]
    half = q_ref.shape[1] // 2
    heads = half // HEAD_DIM
    n_dest = 2 * n_head
    own_tokens = tokens // n_head
    block = own_tokens * heads
    rows = n_dest * block
    width = 2 * block
    scale = math.log2(math.e) / math.sqrt(HEAD_DIM)

    def columns(which, size):
        return pl.ds(pl.multiple_of(which * size, size), size)

    loads = []
    for index, (dst, which) in enumerate(((buf.at[core], core), (other, mate))):
        for part in range(2):
            loads.append(
                pltpu.make_async_copy(
                    kv_ref.at[part, :, columns(which, HEAD_DIM)],
                    dst.at[pl.ds(part * slots, slots)],
                    local_sem.at[2 * index + part],
                )
            )
    loads.append(
        pltpu.make_async_copy(q_ref.at[:, columns(core, half)], qbuf.at[core], local_sem.at[4])
    )
    for copy in loads:
        copy.start()
    fill = fill_ref[0]
    row_ids = lax.broadcasted_iota(jnp.int32, (FILL_ROWS, HEAD_DIM), 0)
    fill_rows = jnp.where(row_ids < 8, lax.div(fill, 8), lax.rem(fill, 8))
    fill_rows = fill_rows.astype(jnp.float32).astype(jnp.bfloat16)
    buf[core, pl.ds(2 * slots, FILL_ROWS)] = fill_rows
    other[pl.ds(2 * slots, FILL_ROWS)] = fill_rows

    barrier = pltpu.get_barrier_semaphore()

    @pl.loop(1, n_ctx)
    def _(step):
        pl.semaphore_signal(
            barrier, inc=1, device_id=(lax.rem(ctx + step, n_ctx), head), device_id_type=MESH
        )

    for step in range(1, n_head):
        for side in range(2):
            pl.semaphore_signal(
                barrier, inc=1, device_id=(2 * group + side, lax.rem(head + step, n_head)),
                device_id_type=MESH,
            )
    pl.semaphore_wait(barrier, n_ctx - 1 + 2 * (n_head - 1))

    q_copy = pltpu.make_async_remote_copy(
        src_ref=q_ref.at[:, columns(mate, half)], dst_ref=qbuf.at[core],
        send_sem=q_send, recv_sem=q_recv,
        device_id=(2 * group + mate, head), device_id_type=MESH,
    )
    q_copy.start()
    for copy in loads[:4]:
        copy.wait()

    def same(step):
        return pltpu.make_async_remote_copy(
            src_ref=buf.at[core], dst_ref=buf.at[core + 2 * step],
            send_sem=kv_send.at[2 * step], recv_sem=kv_recv.at[core + 2 * step],
            device_id=(2 * xor(group, step, n_group) + core, head), device_id_type=MESH,
        )

    def cross(step):
        return pltpu.make_async_remote_copy(
            src_ref=other, dst_ref=buf.at[core + 2 * step],
            send_sem=kv_send.at[2 * step + 1], recv_sem=kv_recv.at[core + 2 * step],
            device_id=(2 * xor(group, step, n_group) + mate, head), device_id_type=MESH,
        )

    cross(0).start()

    @pl.loop(1, n_group)
    def _(step):
        same(step).start()
        cross(step).start()

    loads[4].wait()
    q_copy.wait_recv()
    for dest in range(n_dest):
        side, part = dest // n_head, dest % n_head
        grown = qbuf[side].astype(jnp.float32)
        pieces = [
            grown[part * own_tokens:(part + 1) * own_tokens, i * HEAD_DIM:(i + 1) * HEAD_DIM]
            for i in range(heads)
        ]
        stacked = jnp.concatenate(pieces, axis=0)
        qt[:, dest * block:(dest + 1) * block] = jnp.transpose(stacked).astype(jnp.bfloat16)

    acc[...] = jnp.zeros_like(acc)
    total[...] = jnp.zeros_like(total)
    peak[...] = jnp.full_like(peak, NEG)

    offset = offset_ref[0]
    row = lax.broadcasted_iota(jnp.int32, (1, rows), 1)
    token = lax.div(row, block) * own_tokens + lax.rem(row, own_tokens)
    slot_ids = lax.broadcasted_iota(jnp.int32, (slots, width), 0)

    def chunk(index):
        shard = 2 * xor(group, lax.div(index, 2), n_group) + lax.rem(index, 2)
        keys = buf[index, pl.ds(0, slots)]
        values_t = jnp.transpose(buf[index, pl.ds(slots, slots)])
        info = buf[index, pl.ds(2 * slots, FILL_ROWS)].astype(jnp.float32)
        live = (info[0:1] * 8.0 + info[8:9]).astype(jnp.int32)
        live = jnp.concatenate([live] * (width // HEAD_DIM), axis=1)
        for start in range(0, rows, width):
            here = slice(start, start + width)
            position = offset + tokens * 2 * group + token[:, here] - shard * slots
            last = jnp.minimum(position, live - 1)
            scores = jnp.dot(keys, qt[:, here], preferred_element_type=jnp.float32)
            scores = jnp.where(slot_ids <= last, scores, NEG)
            old = peak[:, here]
            new = jnp.maximum(old, jnp.max(scores, axis=0, keepdims=True))
            fade = jnp.exp2((old - new) * scale)
            weights = jnp.exp2((scores - new) * scale)
            peak[:, here] = new
            total[:, here] = total[:, here] * fade + jnp.sum(weights, axis=0, keepdims=True)
            acc[:, here] = acc[:, here] * fade + jnp.dot(
                values_t, weights.astype(jnp.bfloat16), preferred_element_type=jnp.float32
            )

    def wait_slab(index):
        pltpu.make_async_copy(buf.at[index], buf.at[index], kv_recv.at[index]).wait()

    @pl.loop(0, n_ctx)
    def _(step):
        index = jnp.where(step < 2, lax.rem(core + step, 2), step)

        @pl.when(step > 0)
        def _():
            wait_slab(index)

        chunk(index)

    mine = core * n_head + head
    my_source = head * 2 + core

    def send(dest):
        return pltpu.make_async_remote_copy(
            src_ref=staged.at[dest], dst_ref=landed.at[my_source],
            send_sem=out_send.at[dest], recv_sem=out_recv.at[my_source],
            device_id=(2 * group + lax.div(dest, n_head), lax.rem(dest, n_head)),
            device_id_type=MESH,
        )

    def finished(dest):
        here = columns(dest, block)
        return jnp.transpose(acc[:, here] / total[:, here]).astype(jnp.bfloat16)

    @pl.loop(1, n_dest)
    def _(step):
        dest = lax.rem(mine + step, n_dest)
        staged[dest] = finished(dest)
        send(dest).start()

    landed[my_source] = finished(mine)

    @pl.loop(1, n_dest)
    def _(step):
        source = lax.rem(my_source + step, n_dest)
        pltpu.make_async_copy(landed.at[source], landed.at[source], out_recv.at[source]).wait()

    for source in range(n_dest):
        grown = landed[source].astype(jnp.float32)
        pieces = [grown[i * own_tokens:(i + 1) * own_tokens] for i in range(heads)]
        out_ref[:, source * half:(source + 1) * half] = jnp.concatenate(pieces, axis=1).astype(
            jnp.bfloat16
        )

    q_copy.wait_send()
    cross(0).wait_send()

    @pl.loop(1, n_group)
    def _(step):
        same(step).wait_send()
        cross(step).wait_send()

    @pl.loop(1, n_dest)
    def _(step):
        send(lax.rem(mine + step, n_dest)).wait_send()


def per_device(n_ctx, n_head, queries, kv_cache, fill_len, prompt_offset):
    tokens, feats = queries.shape
    slots = kv_cache.shape[1]
    half = feats // 2
    n_dest = 2 * n_head
    own_tokens = tokens // n_head
    block = own_tokens * (half // HEAD_DIM)
    rows = n_dest * block
    slab = 2 * slots + FILL_ROWS
    bf16, f32 = jnp.bfloat16, jnp.float32
    dma = pltpu.SemaphoreType.DMA
    return pl.pallas_call(
        functools.partial(kernel, n_ctx, n_head),
        out_shape=jax.ShapeDtypeStruct((own_tokens, n_head * feats), bf16),
        in_specs=[
            pl.BlockSpec(memory_space=pltpu.SMEM),
            pl.BlockSpec(memory_space=pltpu.SMEM),
            pl.BlockSpec(memory_space=pl.ANY),
            pl.BlockSpec(memory_space=pl.ANY),
        ],
        out_specs=pl.BlockSpec(memory_space=pltpu.VMEM),
        scratch_shapes=[
            pltpu.VMEM((n_ctx, slab, HEAD_DIM), bf16),
            pltpu.VMEM((slab, HEAD_DIM), bf16),
            pltpu.VMEM((2, tokens, half), bf16),
            pltpu.VMEM((HEAD_DIM, rows), bf16),
            pltpu.VMEM((HEAD_DIM, rows), f32),
            pltpu.VMEM((1, rows), f32),
            pltpu.VMEM((1, rows), f32),
            pltpu.VMEM((n_dest, block, HEAD_DIM), bf16),
            pltpu.VMEM((n_dest, block, HEAD_DIM), bf16),
            dma((5,)), dma, dma, dma((n_ctx,)), dma((n_ctx,)), dma((n_dest,)), dma((n_dest,)),
        ],
        compiler_params=pltpu.CompilerParams(
            collective_id=0, has_side_effects=True, vmem_limit_bytes=48 * 2**20
        ),
    )(fill_len, prompt_offset, queries, kv_cache)


def solution(mesh):
    in_specs = (P("ctx", "head"), P(None, "ctx", "head"), P("ctx"), P())
    out_specs = P(("ctx", "head"), None)
    return jax.shard_map(
        functools.partial(per_device, mesh.shape["ctx"], mesh.shape["head"]),
        mesh=mesh, in_specs=in_specs, out_specs=out_specs, check_vma=False,
    )
```

time: 179 us -> 44.4 us (0.25)
  waiting for transfers between devices: 77.5 us -> 0 us
  Pallas kernels: 0 us -> 40.2 us
  other arithmetic: 32.6 us -> 0 us
  local copies, waits for them, and re-layouts: 25.5 us -> 2.69 us
  matrix products: 17.2 us -> 0 us
  between operations: 14.9 us -> 1.31 us
  starting transfers between devices: 10.4 us -> 0 us
    all_to_all x2 -> x0, waiting for transfers between devices: 47.3 us -> none  [the longest x1 47.3 us: per_device(): lax.all_to_all(partial_value[None], ('ctx', 'head'), split_axis=1, concat...]
    pallas_call x0 -> x1, Pallas kernels: none -> 40.2 us  [per_device(): pl.pallas_call(functools.partial(kernel, n_ctx, n_head), out_shape=jax.Sh...]
    all_gather x1 -> x0, waiting for transfers between devices: 29.5 us -> none  [per_device(): arrived = lax.all_gather(queries, 'ctx', axis=0, tiled=True)]
    dot_general x2 -> x0, matrix products: 17.2 us -> none  [the longest x1 10 us: shard_partial(): jnp.einsum('hgnk,khd->nhgd', rounded, value_block, preferred_element_type...]
    unnamed x2 -> x0, other arithmetic: 14.4 us -> none
    reduce_sum x3 -> x0, other arithmetic: 10.6 us -> none  [the longest x1 9.31 us: shard_partial(): row_sum = jnp.sum(weights, axis=-1)]
    all_to_all x2 -> x0, starting transfers between devices: 10.4 us -> none  [the longest x1 5.84 us: per_device(): lax.all_to_all(partial_value[None], ('ctx', 'head'), split_axis=1, concat...]
    unnamed x8 -> x5, local copies, waits for them, and re-layouts: 13 us -> 2.69 us
  transfers between devices with their start and end apart: 3 -> 0, of which waited for: 2 -> 0; matrix products, arithmetic and copies ran while one was open for 21% -> 0% of each run, Pallas kernels for 0% -> 0%
where the time goes in v1:
time: 44.4 us; the launch traced here: 44.2 us
  Pallas kernels  40.2 us (91%)
  local copies, waits for them, and re-layouts  2.69 us (6%)
  between operations  1.31 us (3%)
    pallas_call x1, Pallas kernels, per_device(): pl.pallas_call(functools.partial(kernel, n_ctx, n_head), out_shape=jax.Sh...  40.2 us
    unnamed x5, local copies, waits for them, and re-layouts  2.69 us

profile of v1, /device:TPU:1, one launch (start us, length us, event | category | flops | bytes accessed | tf_op | source)
XLA Modules:
  0.0 44.2 jit_solution(2881543369416664546)
XLA Ops:
  1.3 0.0 copy-start
  1.3 1.0 %copy-done = bf16[2,512,256]{2,1,0:T(8,128)(2,1)S(1)} copy-done((bf16[2,512,256]{2,1,0:T(8,128)(2,1)S(1)}, bf16[2,512,256]{2,1,0:T(8,128)(2,1)}, u32[]{:S(2)}) %copy-start) | copy-done | bytes 524312
  2.3 0.0 copy-start.1
  2.3 0.9 %copy-done.1 = bf16[32,4096]{1,0:T(8,128)(2,1)S(1)} copy-done((bf16[32,4096]{1,0:T(8,128)(2,1)S(1)}, bf16[32,4096]{1,0:T(8,128)(2,1)}, u32[]{:S(2)}) %copy-start.1) | copy-done | bytes 262168
  3.3 40.2 %shard_map.46 = bf16[8,16384]{1,0:T(8,128)(2,1)S(1)} custom-call(s32[1]{0:T(128)S(6)} %copy.6.fill_ref, s32[1]{0:T(128)S(6)} %copy.7.offset_ref, bf16[32,4096]{1,0:T(8,128)(2,1)S(1)} %copy-done.1, bf16[2,512,256]{2,1,0:T(8,128)(2,1)S(1)} %copy-done), custom_call_target="tpu_custom_call" | custom-call | tf_op jit(solution)/shard_map/pallas_call | solution.py:235
  43.5 0.7 %copy.8 = bf16[8,16384]{1,0:T(8,128)(2,1)} copy(bf16[8,16384]{1,0:T(8,128)(2,1)S(1)} %shard_map.46) | data formatting | bytes 524288
Async XLA Ops:
  1.3 1.0 %copy-start = (bf16[2,512,256]{2,1,0:T(8,128)(2,1)S(1)}, bf16[2,512,256]{2,1,0:T(8,128)(2,1)}, u32[]{:S(2)}) copy-start(bf16[2,512,256]{2,1,0:T(8,128)(2,1)} %kv_ref.1) | copy-start | bytes 1572868
  2.3 0.9 %copy-start.1 = (bf16[32,4096]{1,0:T(8,128)(2,1)S(1)}, bf16[32,4096]{1,0:T(8,128)(2,1)}, u32[]{:S(2)}) copy-start(bf16[32,4096]{1,0:T(8,128)(2,1)} %q_ref.1) | copy-start | bytes 786436

commit v2 on v1

--- a/solution.py
+++ b/solution.py
@@ -43,6 +43,7 @@
     block = own_tokens * heads
     rows = n_dest * block
     width = 2 * block
+    pack = 16 // own_tokens
     scale = math.log2(math.e) / math.sqrt(HEAD_DIM)
 
     def columns(which, size):
@@ -84,6 +85,21 @@
                 barrier, inc=1, device_id=(2 * group + side, lax.rem(head + step, n_head)),
                 device_id_type=MESH,
             )
+
+    def lay_out(side):
+        for part in range(n_head):
+            grown = qbuf[side, pl.ds(part // pack * 16, 16)].astype(jnp.float32)
+            inner = part % pack * own_tokens
+            pieces = [
+                grown[inner:inner + own_tokens, i * HEAD_DIM:(i + 1) * HEAD_DIM]
+                for i in range(heads)
+            ]
+            stacked = jnp.concatenate(pieces, axis=0)
+            here = pl.ds(pl.multiple_of((side * n_head + part) * block, block), block)
+            qt[:, here] = jnp.transpose(stacked).astype(jnp.bfloat16)
+
+    loads[4].wait()
+    lay_out(core)
     pl.semaphore_wait(barrier, n_ctx - 1 + 2 * (n_head - 1))
 
     q_copy = pltpu.make_async_remote_copy(
@@ -111,42 +127,63 @@
 
     cross(0).start()
 
-    @pl.loop(1, n_group)
-    def _(step):
+    relayed = n_group == 4
+    direct = 3 if relayed else n_group
+
+    @pl.loop(1, direct)
+    def _(turn):
+        step = jnp.where(core == 0, direct - turn, turn) if relayed else turn
         same(step).start()
         cross(step).start()
 
-    loads[4].wait()
+    def relay(side):
+        held = 2 * (2 - side) + side
+        return pltpu.make_async_remote_copy(
+            src_ref=buf.at[held], dst_ref=buf.at[6 + side],
+            send_sem=kv_send.at[6 + side], recv_sem=kv_recv.at[6 + side],
+            device_id=(2 * xor(group, 1 + side, n_group) + core, head), device_id_type=MESH,
+        )
+
     q_copy.wait_recv()
-    for dest in range(n_dest):
-        side, part = dest // n_head, dest % n_head
-        grown = qbuf[side].astype(jnp.float32)
-        pieces = [
-            grown[part * own_tokens:(part + 1) * own_tokens, i * HEAD_DIM:(i + 1) * HEAD_DIM]
-            for i in range(heads)
-        ]
-        stacked = jnp.concatenate(pieces, axis=0)
-        qt[:, dest * block:(dest + 1) * block] = jnp.transpose(stacked).astype(jnp.bfloat16)
+    lay_out(mate)
 
     acc[...] = jnp.zeros_like(acc)
     total[...] = jnp.zeros_like(total)
     peak[...] = jnp.full_like(peak, NEG)
 
     offset = offset_ref[0]
-    row = lax.broadcasted_iota(jnp.int32, (1, rows), 1)
-    token = lax.div(row, block) * own_tokens + lax.rem(row, own_tokens)
     slot_ids = lax.broadcasted_iota(jnp.int32, (slots, width), 0)
 
-    def chunk(index):
+    mine = core * n_head + head
+    my_source = head * 2 + core
+
+    def send(dest):
+        return pltpu.make_async_remote_copy(
+            src_ref=staged.at[dest], dst_ref=landed.at[my_source],
+            send_sem=out_send.at[dest], recv_sem=out_recv.at[my_source],
+            device_id=(2 * group + lax.div(dest, n_head), lax.rem(dest, n_head)),
+            device_id_type=MESH,
+        )
+
+    def chunk(index, final):
         shard = 2 * xor(group, lax.div(index, 2), n_group) + lax.rem(index, 2)
         keys = buf[index, pl.ds(0, slots)]
         values_t = jnp.transpose(buf[index, pl.ds(slots, slots)])
         info = buf[index, pl.ds(2 * slots, FILL_ROWS)].astype(jnp.float32)
         live = (info[0:1] * 8.0 + info[8:9]).astype(jnp.int32)
         live = jnp.concatenate([live] * (width // HEAD_DIM), axis=1)
-        for start in range(0, rows, width):
-            here = slice(start, start + width)
-            position = offset + tokens * 2 * group + token[:, here] - shard * slots
+        pairs = n_head // 2
+        for turn in range(2 * pairs):
+            if final:
+                pair = lax.rem(lax.div(head, 2) + 1 + turn // 2, pairs)
+                place = turn % 2 * pairs + pair
+                here = columns(place, width)
+            else:
+                place = turn
+                here = slice(turn * width, (turn + 1) * width)
+            row = place * width + lax.broadcasted_iota(jnp.int32, (1, width), 1)
+            token = lax.div(row, block) * own_tokens + lax.rem(row, own_tokens)
+            position = offset + tokens * 2 * group + token - shard * slots
             last = jnp.minimum(position, live - 1)
             scores = jnp.dot(keys, qt[:, here], preferred_element_type=jnp.float32)
             scores = jnp.where(slot_ids <= last, scores, NEG)
@@ -154,47 +191,54 @@
             new = jnp.maximum(old, jnp.max(scores, axis=0, keepdims=True))
             fade = jnp.exp2((old - new) * scale)
             weights = jnp.exp2((scores - new) * scale)
-            peak[:, here] = new
-            total[:, here] = total[:, here] * fade + jnp.sum(weights, axis=0, keepdims=True)
-            acc[:, here] = acc[:, here] * fade + jnp.dot(
+            sums = total[:, here] * fade + jnp.sum(weights, axis=0, keepdims=True)
+            out = acc[:, here] * fade + jnp.dot(
                 values_t, weights.astype(jnp.bfloat16), preferred_element_type=jnp.float32
             )
+            if not final:
+                peak[:, here] = new
+                total[:, here] = sums
+                acc[:, here] = out
+                continue
+            done = jnp.transpose(out / sums).astype(jnp.bfloat16)
+            for part in range(2):
+                dest = 2 * place + part
+                piece = done[part * block:(part + 1) * block]
+
+                @pl.when(dest != mine)
+                def _(dest=dest, piece=piece):
+                    staged[dest] = piece
+                    send(dest).start()
+
+                @pl.when(dest == mine)
+                def _(piece=piece):
+                    landed[my_source] = piece
 
     def wait_slab(index):
         pltpu.make_async_copy(buf.at[index], buf.at[index], kv_recv.at[index]).wait()
 
-    @pl.loop(0, n_ctx)
+    @pl.loop(0, n_ctx - 1)
     def _(step):
         index = jnp.where(step < 2, lax.rem(core + step, 2), step)
-
-        @pl.when(step > 0)
+        waits = step > 0
+        if relayed:
+            index = jnp.where(step == 2, 3, jnp.where(step == 3, 4, jnp.where(step == 4, 2, index)))
+            waits = (step == 1) | (step > 3)
+
+            @pl.when(step == 2)
+            def _():
+                for side in range(2):
+                    wait_slab(2 * (2 - side) + side)
+                    relay(side).start()
+
+        @pl.when(waits)
         def _():
             wait_slab(index)
 
-        chunk(index)
-
-    mine = core * n_head + head
-    my_source = head * 2 + core
-
-    def send(dest):
-        return pltpu.make_async_remote_copy(
-            src_ref=staged.at[dest], dst_ref=landed.at[my_source],
-            send_sem=out_send.at[dest], recv_sem=out_recv.at[my_source],
-            device_id=(2 * group + lax.div(dest, n_head), lax.rem(dest, n_head)),
-            device_id_type=MESH,
-        )
-
-    def finished(dest):
-        here = columns(dest, block)
-        return jnp.transpose(acc[:, here] / total[:, here]).astype(jnp.bfloat16)
-
-    @pl.loop(1, n_dest)
-    def _(step):
-        dest = lax.rem(mine + step, n_dest)
-        staged[dest] = finished(dest)
-        send(dest).start()
-
-    landed[my_source] = finished(mine)
+        chunk(index, False)
+
+    wait_slab(n_ctx - 1)
+    chunk(n_ctx - 1, True)
 
     @pl.loop(1, n_dest)
     def _(step):
@@ -211,10 +255,14 @@
     q_copy.wait_send()
     cross(0).wait_send()
 
-    @pl.loop(1, n_group)
+    @pl.loop(1, direct)
     def _(step):
         same(step).wait_send()
         cross(step).wait_send()
+
+    if relayed:
+        for side in range(2):
+            relay(side).wait_send()
 
     @pl.loop(1, n_dest)
     def _(step):
@@ -238,8 +286,8 @@
         in_specs=[
             pl.BlockSpec(memory_space=pltpu.SMEM),
             pl.BlockSpec(memory_space=pltpu.SMEM),
-            pl.BlockSpec(memory_space=pl.ANY),
-            pl.BlockSpec(memory_space=pl.ANY),
+            pl.BlockSpec(memory_space=pltpu.HBM),
+            pl.BlockSpec(memory_space=pltpu.HBM),
         ],
         out_specs=pl.BlockSpec(memory_space=pltpu.VMEM),
         scratch_shapes=[

time: 44.4 us -> 39.8 us (0.90)
  Pallas kernels: 40.2 us -> 35.6 us
    pallas_call x1, Pallas kernels: 40.2 us -> 35.6 us  [per_device(): pl.pallas_call(functools.partial(kernel, n_ctx, n_head), out_shape=jax.Sh...]
where the time goes in v2:
time: 39.8 us; the launch traced here: 39.6 us
  Pallas kernels  35.6 us (89%)
  local copies, waits for them, and re-layouts  2.69 us (7%)
  between operations  1.31 us (3%)
    pallas_call x1, Pallas kernels, per_device(): pl.pallas_call(functools.partial(kernel, n_ctx, n_head), out_shape=jax.Sh...  35.6 us
    unnamed x5, local copies, waits for them, and re-layouts  2.69 us

profile of v2, /device:TPU:1, one launch (start us, length us, event | category | flops | bytes accessed | tf_op | source)
XLA Modules:
  0.0 39.6 jit_solution(7085037097951236173)
XLA Ops:
  1.3 0.0 copy-start
  1.3 1.0 %copy-done = bf16[2,512,256]{2,1,0:T(8,128)(2,1)S(1)} copy-done((bf16[2,512,256]{2,1,0:T(8,128)(2,1)S(1)}, bf16[2,512,256]{2,1,0:T(8,128)(2,1)}, u32[]{:S(2)}) %copy-start) | copy-done | bytes 524312
  2.3 0.0 copy-start.1
  2.3 0.9 %copy-done.1 = bf16[32,4096]{1,0:T(8,128)(2,1)S(1)} copy-done((bf16[32,4096]{1,0:T(8,128)(2,1)S(1)}, bf16[32,4096]{1,0:T(8,128)(2,1)}, u32[]{:S(2)}) %copy-start.1) | copy-done | bytes 262168
  3.3 35.6 %shard_map.46 = bf16[8,16384]{1,0:T(8,128)(2,1)S(1)} custom-call(s32[1]{0:T(128)S(6)} %copy.6.fill_ref, s32[1]{0:T(128)S(6)} %copy.7.offset_ref, bf16[32,4096]{1,0:T(8,128)(2,1)S(1)} %copy-done.1, bf16[2,512,256]{2,1,0:T(8,128)(2,1)S(1)} %copy-done), custom_call_target="tpu_custom_call" | custom-call | tf_op jit(solution)/shard_map/pallas_call | solution.py:283
  38.9 0.7 %copy.8 = bf16[8,16384]{1,0:T(8,128)(2,1)} copy(bf16[8,16384]{1,0:T(8,128)(2,1)S(1)} %shard_map.46) | data formatting | bytes 524288
Async XLA Ops:
  1.3 1.0 %copy-start = (bf16[2,512,256]{2,1,0:T(8,128)(2,1)S(1)}, bf16[2,512,256]{2,1,0:T(8,128)(2,1)}, u32[]{:S(2)}) copy-start(bf16[2,512,256]{2,1,0:T(8,128)(2,1)} %kv_ref.1) | copy-start | bytes 1572868
  2.3 0.9 %copy-start.1 = (bf16[32,4096]{1,0:T(8,128)(2,1)S(1)}, bf16[32,4096]{1,0:T(8,128)(2,1)}, u32[]{:S(2)}) copy-start(bf16[32,4096]{1,0:T(8,128)(2,1)} %q_ref.1) | copy-start | bytes 786436

commit v3 on v2

--- a/solution.py
+++ b/solution.py
@@ -24,9 +24,9 @@
 
 
 def kernel(
-    n_ctx, n_head, fill_ref, offset_ref, q_ref, kv_ref, out_ref,
+    n_ctx, n_head, fill_hbm, offset_hbm, q_ref, kv_ref, out_ref,
     buf, other, qbuf, qt, acc, peak, total, staged, landed,
-    local_sem, q_send, q_recv, kv_send, kv_recv, out_send, out_recv,
+    fill_ref, offset_ref, local_sem, q_send, q_recv, kv_send, kv_recv, out_send, out_recv,
 ):
     ctx = lax.axis_index("ctx")
     head = lax.axis_index("head")
@@ -42,13 +42,18 @@
     own_tokens = tokens // n_head
     block = own_tokens * heads
     rows = n_dest * block
-    width = 2 * block
     pack = 16 // own_tokens
     scale = math.log2(math.e) / math.sqrt(HEAD_DIM)
 
     def columns(which, size):
         return pl.ds(pl.multiple_of(which * size, size), size)
 
+    scalars = [
+        pltpu.make_async_copy(fill_hbm, fill_ref, local_sem.at[5]),
+        pltpu.make_async_copy(offset_hbm, offset_ref, local_sem.at[6]),
+    ]
+    for copy in scalars:
+        copy.start()
     loads = []
     for index, (dst, which) in enumerate(((buf.at[core], core), (other, mate))):
         for part in range(2):
@@ -64,13 +69,6 @@
     )
     for copy in loads:
         copy.start()
-    fill = fill_ref[0]
-    row_ids = lax.broadcasted_iota(jnp.int32, (FILL_ROWS, HEAD_DIM), 0)
-    fill_rows = jnp.where(row_ids < 8, lax.div(fill, 8), lax.rem(fill, 8))
-    fill_rows = fill_rows.astype(jnp.float32).astype(jnp.bfloat16)
-    buf[core, pl.ds(2 * slots, FILL_ROWS)] = fill_rows
-    other[pl.ds(2 * slots, FILL_ROWS)] = fill_rows
-
     barrier = pltpu.get_barrier_semaphore()
 
     @pl.loop(1, n_ctx)
@@ -98,6 +96,14 @@
             here = pl.ds(pl.multiple_of((side * n_head + part) * block, block), block)
             qt[:, here] = jnp.transpose(stacked).astype(jnp.bfloat16)
 
+    for copy in scalars:
+        copy.wait()
+    fill = fill_ref[0]
+    row_ids = lax.broadcasted_iota(jnp.int32, (FILL_ROWS, HEAD_DIM), 0)
+    fill_rows = jnp.where(row_ids < 8, lax.div(fill, 8), lax.rem(fill, 8))
+    fill_rows = fill_rows.astype(jnp.float32).astype(jnp.bfloat16)
+    buf[core, pl.ds(2 * slots, FILL_ROWS)] = fill_rows
+    other[pl.ds(2 * slots, FILL_ROWS)] = fill_rows
     loads[4].wait()
     lay_out(core)
     pl.semaphore_wait(barrier, n_ctx - 1 + 2 * (n_head - 1))
@@ -152,7 +158,6 @@
     peak[...] = jnp.full_like(peak, NEG)
 
     offset = offset_ref[0]
-    slot_ids = lax.broadcasted_iota(jnp.int32, (slots, width), 0)
 
     mine = core * n_head + head
     my_source = head * 2 + core
@@ -171,9 +176,11 @@
         values_t = jnp.transpose(buf[index, pl.ds(slots, slots)])
         info = buf[index, pl.ds(2 * slots, FILL_ROWS)].astype(jnp.float32)
         live = (info[0:1] * 8.0 + info[8:9]).astype(jnp.int32)
+        pairs = n_head // 2
+        width = 2 * block if final else rows
         live = jnp.concatenate([live] * (width // HEAD_DIM), axis=1)
-        pairs = n_head // 2
-        for turn in range(2 * pairs):
+        slot_ids = lax.broadcasted_iota(jnp.int32, (slots, width), 0)
+        for turn in range(rows // width):
             if final:
                 pair = lax.rem(lax.div(head, 2) + 1 + turn // 2, pairs)
                 place = turn % 2 * pairs + pair
@@ -284,8 +291,8 @@
         functools.partial(kernel, n_ctx, n_head),
         out_shape=jax.ShapeDtypeStruct((own_tokens, n_head * feats), bf16),
         in_specs=[
-            pl.BlockSpec(memory_space=pltpu.SMEM),
-            pl.BlockSpec(memory_space=pltpu.SMEM),
+            pl.BlockSpec(memory_space=pltpu.HBM),
+            pl.BlockSpec(memory_space=pltpu.HBM),
             pl.BlockSpec(memory_space=pltpu.HBM),
             pl.BlockSpec(memory_space=pltpu.HBM),
         ],
@@ -300,10 +307,12 @@
             pltpu.VMEM((1, rows), f32),
             pltpu.VMEM((n_dest, block, HEAD_DIM), bf16),
             pltpu.VMEM((n_dest, block, HEAD_DIM), bf16),
-            dma((5,)), dma, dma, dma((n_ctx,)), dma((n_ctx,)), dma((n_dest,)), dma((n_dest,)),
+            pltpu.SMEM((1,), jnp.int32),
+            pltpu.SMEM((1,), jnp.int32),
+            dma((7,)), dma, dma, dma((n_ctx,)), dma((n_ctx,)), dma((n_dest,)), dma((n_dest,)),
         ],
         compiler_params=pltpu.CompilerParams(
-            collective_id=0, has_side_effects=True, vmem_limit_bytes=48 * 2**20
+            collective_id=0, has_side_effects=True, vmem_limit_bytes=63 * 2**20
         ),
     )(fill_len, prompt_offset, queries, kv_cache)
 

time: 39.8 us -> 37.4 us (0.940)
  Pallas kernels: 35.6 us -> 34.3 us
  local copies, waits for them, and re-layouts: 2.69 us -> 1.67 us
    pallas_call x1, Pallas kernels: 35.6 us -> 34.3 us  [per_device(): pl.pallas_call(functools.partial(kernel, n_ctx, n_head), out_shape=jax.Sh...]
    unnamed x5 -> x1, local copies, waits for them, and re-layouts: 2.69 us -> 1.67 us
where the time goes in v3:
time: 37.4 us; the launch traced here: 37.2 us
  Pallas kernels  34.3 us (92%)
  local copies, waits for them, and re-layouts  1.67 us (4%)
  between operations  1.3 us (3%)
    pallas_call x1, Pallas kernels, per_device(): pl.pallas_call(functools.partial(kernel, n_ctx, n_head), out_shape=jax.Sh...  34.3 us
    unnamed x1, local copies, waits for them, and re-layouts  1.67 us

profile of v3, /device:TPU:1, one launch (start us, length us, event | category | flops | bytes accessed | tf_op | source)
XLA Modules:
  0.0 37.2 jit_solution(14080082056345756942)
XLA Ops:
  1.3 34.3 %shard_map.46 = bf16[8,16384]{1,0:T(8,128)(2,1)} custom-call(s32[1]{0:T(128)S(6)} %copy.6.fill_hbm, s32[1]{0:T(128)S(6)} %copy.7.offset_hbm, bf16[32,4096]{1,0:T(8,128)(2,1)} %q_ref.1, bf16[2,512,256]{2,1,0:T(8,128)(2,1)} %kv_ref.1), custom_call_target="tpu_custom_call" | custom-call | tf_op jit(solution)/shard_map/pallas_call | solution.py:290
  35.6 1.7 %copy.8 = bf16[8,16384]{1,0:T(8,128)(2,1)} copy(bf16[8,16384]{1,0:T(8,128)(2,1)} %shard_map.46) | data formatting | bytes 524288
